TPU v7x, 32 devices: a whole 2x2x4 slice. The times are simulated.
32 devices in a mesh: space: 16 (over z, x, core), spec: 2 (over y).
Axes of the slice: x: 2, y: 2, z: 4, core: 2. Of those that a mesh axis runs over, the one named last changes fastest.
Arguments:
- tracers: float32 [240, 8, 128, 384], P('spec', None, 'space'), may hold values from 0.1 to 10
- courant: float32 [2, 8, 128, 384], P(None, None, 'space'), may hold values from -0.9 to 0.9
- layer_mass: float32 [8, 128, 384], P(None, 'space'), may hold values from 0.5 to 2
- pbl_top: int32 [128, 384], P('space'), may hold values from 1 to 8
- land_type: int32 [128, 384], P('space'), may hold values from 0 to 10
- rates: float32 [11, 240], replicated, may hold values from 0.05 to 3
- coupling: float32 [240, 240], replicated, may hold values from -0.375 to 0.375
Outputs:
- updated: float32 [240, 8, 128, 384], P('spec', None, 'space')
- deposited: float32 [240, 128, 384], P('spec', 'space')
All inputs are finite; a program needn't handle non-finite values.
Results may differ from a plain program's by a relative error of at most 0.0003.
Values sent between devices are 32-bit elements; how exact they have to be, the bound alone decides.
A program may use at most 192 MiB of HBM per device.

v0:
```python
import jax
import jax.numpy as jnp
from jax import lax
from jax.sharding import PartitionSpec as P

STEPS = 2


def padded_2(array, sides, width):
    for axis, dim in sides:
        devices, length = (lax.axis_size(axis), array.shape[dim])
        up = [(i, (i + 1) % devices) for i in range(devices - 1)]
        down = [(j, i) for i, j in up]
        last = lax.slice_in_dim(array, length - width, length, axis=dim)
        leading = lax.slice_in_dim(array, 0, width, axis=dim)
        before = lax.ppermute(last, axis, up)
        after = lax.ppermute(leading, axis, down)
        array = jnp.concatenate([before, array, after], axis=dim)
    return array


def sweep(field, speed, axis):
    count = field.shape[axis]

    def cut(a, lo, hi):
        return lax.slice_in_dim(a, lo, hi, axis=axis)

    edge = 7.0 / 12.0 * (cut(field, 1, count - 2) + cut(field, 2, count - 1)) - 1.0 / 12.0 * (
        cut(field, 0, count - 3) + cut(field, 3, count)
    )
    lower = cut(edge, 0, count - 4)
    upper = cut(edge, 1, count - 3)
    centre = cut(field, 2, count - 2)
    slope = upper - lower
    curve = 6.0 * (centre - 0.5 * (lower + upper))
    cells = count - 4
    face = cut(speed, 3, count - 2)
    upwind = face * (
        cut(upper, 0, cells - 1)
        - 0.5
        * face
        * (cut(slope, 0, cells - 1) - (1.0 - 2.0 * face / 3.0) * cut(curve, 0, cells - 1))
    )
    downwind = face * (
        cut(lower, 1, cells)
        - 0.5 * face * (cut(slope, 1, cells) + (1.0 + 2.0 * face / 3.0) * cut(curve, 1, cells))
    )
    flux = jnp.where(face >= 0.0, upwind, downwind)
    return cut(field, 3, count - 3) - (cut(flux, 1, count - 5) - cut(flux, 0, count - 6))


def across(field, speed):
    padded = jnp.pad(field, ((0, 0), (0, 0), (0, 0), (3, 3)))
    return sweep(padded, jnp.pad(speed, ((0, 0), (0, 0), (3, 3))), -1)


def mixing(field, layer_mass, pbl_top):
    levels = jnp.arange(field.shape[1], dtype=jnp.int32)[:, None, None]
    inside = levels < pbl_top[None]
    weights = jnp.where(inside, layer_mass, 0.0)
    average = jnp.sum(weights[None] * field, axis=1) / jnp.sum(weights, axis=0)[None]
    return jnp.where(inside[None], average[:, None], field)


def deposit(field, surface_mass, land_type, rates):
    kinds = jnp.arange(rates.shape[0], dtype=jnp.int32)[:, None]
    onehot = (land_type.reshape(1, -1) == kinds).astype(jnp.float32)
    loss = jnp.dot(rates.T, onehot, precision=lax.Precision.HIGHEST).reshape(
        field.shape[0], field.shape[2], field.shape[3]
    )
    bottom = field[:, 0]
    kept = bottom * jnp.exp(-loss)
    return (field.at[:, 0].set(kept), (bottom - kept) * surface_mass[None])


def on_device(tracers, courant, layer_mass, pbl_top, land_type, rates, coupling):
    field = tracers
    for step in range(STEPS):
        padded, speed = (padded_2(field, (("space", 2),), 3), padded_2(courant, (("space", 2),), 3))
        field = sweep(padded, speed[0], -2)
        field = across(field, courant[1])
    gathered = lax.all_to_all(field, "spec", split_axis=2, concat_axis=0, tiled=True)
    part = gathered.shape[2]
    start_row = lax.axis_index("spec") * part
    mass = lax.dynamic_slice_in_dim(layer_mass, start_row, part, 1)
    tops = lax.dynamic_slice_in_dim(pbl_top, start_row, part, 0)
    kinds = lax.dynamic_slice_in_dim(land_type, start_row, part, 0)
    mixed = mixing(gathered, mass, tops)
    coupled = mixed + jnp.dot(
        coupling, mixed.reshape(mixed.shape[0], -1), precision=lax.Precision.HIGHEST
    ).reshape(mixed.shape)
    column_out, column_flux = deposit(coupled, mass[0], kinds, rates)
    updated, returned = (
        lax.all_to_all(column_out, "spec", split_axis=0, concat_axis=2, tiled=True),
        lax.all_to_all(column_flux[:, None], "spec", split_axis=0, concat_axis=2, tiled=True),
    )
    deposited = returned[:, 0]
    return (updated, deposited)


def solution(mesh):
    return jax.shard_map(
        on_device,
        mesh=mesh,
        in_specs=(
            P("spec", None, "space", None),
            P(None, None, "space", None),
            P(None, "space", None),
            P("space", None),
            P("space", None),
            P(),
            P(),
        ),
        out_specs=(P("spec", None, "space", None), P("spec", "space", None)),
        check_vma=False,
    )
```

profile of v0, /device:TPU:24, one launch (start us, length us, event | category | flops | bytes accessed | tf_op | source)
XLA Modules:
  0.0 1024.5 jit_solution(1370192616725490134)
XLA Ops:
  32.2 40.6 %collective-permute-done = f32[2,8,3,384]{3,1,2,0:T(8,128)S(1)} collective-permute-done((f32[2,8,3,384]{3,1,2,0:T(8,128)S(1)}, f32[2,8,3,384]{3,1,2,0:T(8,128)S(1)}, u32[]{:S(2)}, u32[]{:S(2)}) %collective-permute-start) | collective-permute-done | bytes 73760 | tf_op jit(solution)/shard_map/ppermute | solution.py:16
  93.2 27.4 %fusion.3 = f32[120,8,11,384]{3,1,2,0:T(8,128)} fusion(f32[120,8,14,384]{3,1,2,0:T(8,128)} %constant_dynamic-update-slice_fusion, f32[120,8,8,384]{3,1,2,0:T(8,128)} %copy.46, f32[120,8,3,384]{3,1,2,0:T(8,128)S(1)} %collective-permute-done.2, f32[120,8,3,384]{3,1,2,0:T(8,128)} %collective-permute-done.3), kind=kLoop, calls=%fused_computation.16 | loop fusion | flops 28385280 | bytes 69304320 | tf_op jit(solution)/shard_map/sub | solution.py:28
  120.7 25.6 %slice_subtract_fusion.5 = (f32[120,8,10,384]{3,1,2,0:T(8,128)}, f32[120,8,10,384]{3,1,2,0:T(8,128)}) fusion(f32[120,8,11,384]{3,1,2,0:T(8,128)} %fusion.3, f32[120,8,14,384]{3,1,2,0:T(8,128)} %constant_dynamic-update-slice_fusion), kind=kLoop, calls=%fused_computation.65 | loop fusion | flops 18432000 | bytes 73728000 | tf_op jit(solution)/shard_map/sub | solution.py:34
  146.3 27.0 %fusion.53 = f32[120,8,9,384]{3,1,2,0:T(8,128)} fusion(f32[120,8,10,384]{3,1,2,0:T(8,128)} %get-tuple-element.19, f32[120,8,10,384]{3,1,2,0:T(8,128)} %get-tuple-element.18, f32[120,8,11,384]{3,1,2,0:T(8,128)} %fusion.3, f32[8,9,384]{2,0,1:T(8,128)S(1)} %get-tuple-element.37, f32[8,9,384]{2,0,1:T(8,128)S(1)} %get-tuple-element.36, ...), kind=kLoop, calls=%fused_computation.82 | loop fusion | flops 36495360 | bytes 80096256 | tf_op jit(solution)/shard_map/jit(_where)/select_n | solution.py:48
  173.3 15.0 %fusion.61 = f32[120,8,8,384]{3,1,2,0:T(8,128)} fusion(f32[120,8,9,384]{3,1,2,0:T(8,128)} %fusion.53, f32[120,8,8,384]{3,2,1,0:T(8,128)S(1)} %bitcast.42), kind=kLoop, calls=%fused_computation.95 | loop fusion | flops 5898240 | bytes 47185920 | tf_op jit(solution)/shard_map/sub | solution.py:49
  188.3 25.0 %fusion.8 = f32[120,8,8,387]{3,1,2,0:T(8,128)S(1)} fusion(f32[120,8,8,384]{3,1,2,0:T(8,128)} %fusion.61), kind=kLoop, calls=%fused_computation.24 | loop fusion | flops 14860800 | bytes 23685120 | tf_op jit(solution)/shard_map/sub | solution.py:28
  213.3 19.8 %slice_subtract_fusion.1 = (f32[120,8,8,386]{3,1,2,0:T(8,128)}, f32[120,8,8,386]{3,1,2,0:T(8,128)}) fusion(f32[120,8,8,387]{3,1,2,0:T(8,128)S(1)} %fusion.8, f32[120,8,8,384]{3,1,2,0:T(8,128)} %fusion.61), kind=kLoop, calls=%fused_computation.59 | loop fusion | flops 14822400 | bytes 59228160 | tf_op jit(solution)/shard_map/sub | solution.py:34
  233.1 33.2 %fusion.33 = f32[120,8,8,385]{3,1,2,0:T(8,128)} fusion(f32[120,8,8,386]{3,1,2,0:T(8,128)} %get-tuple-element.23, f32[120,8,8,386]{3,1,2,0:T(8,128)} %get-tuple-element.22, f32[120,8,8,387]{3,1,2,0:T(8,128)} %copy-done.3, f32[8,8,385]{2,0,1:T(8,128)S(1)} %copy.51, f32[8,8,385]{2,0,1:T(8,128)S(1)} %copy.50, f32[8,8,385]{2,0,1:T(8,128)S(1)} %copy.49, ...), kind=kLoop, calls=%fused_computation.52 | loop fusion | flops 32524800 | bytes 71382080 | tf_op jit(solution)/shard_map/jit(_where)/select_n | solution.py:48
  284.6 47.9 %collective-permute-start.4 = (f32[120,8,3,384]{3,1,2,0:T(8,128)}, f32[120,8,3,384]{3,1,2,0:T(8,128)S(1)}, u32[]{:S(2)}, u32[]{:S(2)}) collective-permute-start(f32[120,8,3,384]{3,1,2,0:T(8,128)} %get-tuple-element.28), channel_id=1, source_target_pairs={{0,2},{2,4},{4,6},{6,8},{8,10},{10,12},{12,14},{14,16},{16,18},{18... | collective-permute-start | bytes 13271048 | tf_op jit(solution)/shard_map/ppermute | solution.py:16
  339.8 43.4 %collective-permute-done.5 = f32[120,8,3,384]{3,1,2,0:T(8,128)S(1)} collective-permute-done((f32[120,8,3,384]{3,1,2,0:T(8,128)}, f32[120,8,3,384]{3,1,2,0:T(8,128)S(1)}, u32[]{:S(2)}, u32[]{:S(2)}) %collective-permute-start.5) | collective-permute-done | bytes 4423712 | tf_op jit(solution)/shard_map/ppermute | solution.py:17
  392.9 27.3 %fusion.1 = f32[120,8,11,384]{3,1,2,0:T(8,128)} fusion(f32[120,8,14,384]{3,1,2,0:T(8,128)} %pad_maximum_fusion, f32[120,8,8,384]{3,1,2,0:T(8,128)} %copy-done.1, f32[120,8,3,384]{3,1,2,0:T(8,128)S(1)} %collective-permute-done.4, f32[120,8,3,384]{3,1,2,0:T(8,128)} %copy-done.5), kind=kLoop, calls=%fused_computation.13 | loop fusion | flops 28385280 | bytes 69304320 | tf_op jit(solution)/shard_map/sub | solution.py:28
  420.2 25.6 %slice_subtract_fusion.4 = (f32[120,8,10,384]{3,1,2,0:T(8,128)}, f32[120,8,10,384]{3,1,2,0:T(8,128)}) fusion(f32[120,8,11,384]{3,1,2,0:T(8,128)} %fusion.1, f32[120,8,14,384]{3,1,2,0:T(8,128)} %pad_maximum_fusion), kind=kLoop, calls=%fused_computation.64 | loop fusion | flops 18432000 | bytes 73728000 | tf_op jit(solution)/shard_map/sub | solution.py:34
  445.8 27.0 %fusion.44 = f32[120,8,9,384]{3,1,2,0:T(8,128)} fusion(f32[120,8,10,384]{3,1,2,0:T(8,128)} %get-tuple-element.17, f32[120,8,10,384]{3,1,2,0:T(8,128)} %get-tuple-element.16, f32[120,8,11,384]{3,1,2,0:T(8,128)} %fusion.1, f32[8,9,384]{2,0,1:T(8,128)S(1)} %get-tuple-element.37, f32[8,9,384]{2,0,1:T(8,128)S(1)} %get-tuple-element.36, ...), kind=kLoop, calls=%fused_computation.71 | loop fusion | flops 36495360 | bytes 80096256 | tf_op jit(solution)/shard_map/jit(_where)/select_n | solution.py:48
  486.7 25.0 %fusion.15 = f32[120,8,8,387]{3,1,2,0:T(8,128)S(1)} fusion(f32[120,8,8,384]{3,1,2,0:T(8,128)} %fusion.59), kind=kLoop, calls=%fused_computation.31 | loop fusion | flops 14860800 | bytes 23685120 | tf_op jit(solution)/shard_map/sub | solution.py:28
  511.7 19.8 %slice_subtract_fusion = (f32[120,8,8,386]{3,1,2,0:T(8,128)}, f32[120,8,8,386]{3,1,2,0:T(8,128)}) fusion(f32[120,8,8,387]{3,1,2,0:T(8,128)S(1)} %fusion.15, f32[120,8,8,384]{3,1,2,0:T(8,128)} %fusion.59), kind=kLoop, calls=%fused_computation.58 | loop fusion | flops 14822400 | bytes 59228160 | tf_op jit(solution)/shard_map/sub | solution.py:34
  531.5 33.1 %fusion.24 = f32[120,8,8,385]{3,1,2,0:T(8,128)} fusion(f32[120,8,8,386]{3,1,2,0:T(8,128)} %get-tuple-element.21, f32[120,8,8,386]{3,1,2,0:T(8,128)} %get-tuple-element.20, f32[120,8,8,387]{3,1,2,0:T(8,128)} %copy-done.2, f32[8,8,385]{2,0,1:T(8,128)S(1)} %copy.51, f32[8,8,385]{2,0,1:T(8,128)S(1)} %copy.50, f32[8,8,385]{2,0,1:T(8,128)S(1)} %copy.49, ...), kind=kLoop, calls=%fused_computation.41 | loop fusion | flops 32524800 | bytes 71382080 | tf_op jit(solution)/shard_map/jit(_where)/select_n | solution.py:48
  564.6 18.6 %fusion.58 = f32[120,8,8,384]{3,1,2,0:T(8,128)} fusion(f32[120,8,8,384]{3,1,2,0:T(8,128)} %fusion.59, f32[120,8,8,385]{3,1,2,0:T(8,128)} %fusion.24), kind=kLoop, calls=%fused_computation.89 | loop fusion | flops 5898240 | bytes 47185920 | tf_op jit(solution)/shard_map/sub | solution.py:49
  603.5 126.4 %all-to-all-done = f32[120,8,8,384]{3,1,0,2:T(8,128)} async-done(((f32[120,8,8,384]{3,1,0,2:T(8,128)}), f32[120,8,8,384]{3,1,0,2:T(8,128)}, u32[]{:S(2)}, u32[]{:S(2)}) %all-to-all-start) | async-done | bytes 11796512 | tf_op jit(solution)/shard_map/all_to_all | solution.py:82
  729.9 15.7 %copy.66 = f32[120,8,2,4,384]{4,3,1,0,2:T(4,128)} copy(f32[120,8,2,4,384]{4,1,0,3,2:T(8,128)} %bitcast.2) | data formatting | bytes 23592960 | tf_op jit(solution)/shard_map/all_to_all | solution.py:82
  794.7 18.5 %convolution_bitcast_fusion = f32[240,12288]{1,0:T(8,128)} fusion(f32[240,240]{1,0:T(8,128)S(1)} %copy-done, f32[240,12288]{1,0:T(8,128)} %broadcast_in_dim.34, f32[240,12288]{1,0:T(8,128)} %all_to_all.43, pred[12288]{0:T(1024)(128)(4,1)S(1)} %lt.30), kind=kOutput, calls=%fused_computation.21 | convolution fusion | flops 8496414720 | bytes 35632128 | tf_op jit(solution)/shard_map/dot_general | solution.py:89
  813.2 14.3 %reshape.92 = f32[240,8,4,384]{3,2,1,0:T(4,128)} reshape(f32[240,12288]{1,0:T(8,128)} %convolution_bitcast_fusion) | data formatting | bytes 23592960 | tf_op jit(solution)/shard_map/reshape | solution.py:91
  839.5 21.9 %all_to_all.54 = f32[240,1,4,384]{3,2,1,0:T(4,128)S(1)} all-to-all(f32[240,1,4,384]{3,2,1,0:T(4,128)S(1)} %get-tuple-element.24), channel_id=1, replica_groups=mesh['space'=16,'spec'=2] {'spec'}, dimensions={0} | all-to-all | bytes 2949120 | tf_op jit(solution)/shard_map/all_to_all | solution.py:95
  871.5 127.5 %all-to-all-done.1 = f32[240,8,4,384]{3,2,1,0:T(4,128)} async-done(((f32[240,8,4,384]{3,2,1,0:T(4,128)}), f32[240,8,4,384]{3,2,1,0:T(4,128)}, u32[]{:S(2)}, u32[]{:S(2)}) %all-to-all-start.1) | async-done | bytes 11796512 | tf_op jit(solution)/shard_map/all_to_all | solution.py:94
  1009.6 14.5 %all_to_all.47 = f32[120,8,8,384]{3,2,1,0:T(8,128)} reshape(f32[120,8,2,4,384]{4,3,2,1,0:T(4,128)} %bitcast.44) | data formatting | bytes 23592960 | tf_op jit(solution)/shard_map/all_to_all | solution.py:94
  (91 shorter events, 202.8 us)
Async XLA Ops:
  0.6 794.1 %copy-start = (f32[240,240]{1,0:T(8,128)S(1)}, f32[240,240]{1,0:T(8,128)}, u32[]{:S(2)}) copy-start(f32[240,240]{1,0:T(8,128)} %param.15) | copy-start | bytes 691204
  12.3 12.8 %copy-start.7 = (f32[2,8,8,384]{3,2,1,0:T(8,128)S(1)}, f32[2,8,8,384]{3,2,1,0:T(8,128)}, u32[]{:S(2)}) copy-start(f32[2,8,8,384]{3,2,1,0:T(8,128)} %param.10) | copy-start | bytes 589828
  18.7 56.1 %collective-permute-start.2 = (f32[120,8,3,384]{3,1,2,0:T(8,128)S(1)}, f32[120,8,3,384]{3,1,2,0:T(8,128)S(1)}, u32[]{:S(2)}, u32[]{:S(2)}) collective-permute-start(f32[120,8,3,384]{3,1,2,0:T(8,128)S(1)} %get-tuple-element.31), channel_id=1, source_target_pairs={{0,2},{2,4},{4,6},{6,8},{8,10},{10,12},{12,14},{14,16},{16,18},{18... | collective-permute-start | bytes 13271048 | tf_op jit(solution)/shard_map/ppermute | solution.py:16
  20.6 68.0 %collective-permute-start.3 = (f32[120,8,3,384]{3,1,2,0:T(8,128)}, f32[120,8,3,384]{3,1,2,0:T(8,128)}, u32[]{:S(2)}, u32[]{:S(2)}) collective-permute-start(f32[120,8,3,384]{3,1,2,0:T(8,128)} %get-tuple-element.30), channel_id=1, source_target_pairs={{2,0},{4,2},{6,4},{8,6},{10,8},{12,10},{14,12},{16,14},{18,16},{20... | collective-permute-start | bytes 13271048 | tf_op jit(solution)/shard_map/ppermute | solution.py:17
  25.2 47.5 %collective-permute-start = (f32[2,8,3,384]{3,1,2,0:T(8,128)S(1)}, f32[2,8,3,384]{3,1,2,0:T(8,128)S(1)}, u32[]{:S(2)}, u32[]{:S(2)}) collective-permute-start(f32[2,8,3,384]{3,1,2,0:T(8,128)S(1)} %get-tuple-element.32), channel_id=1, source_target_pairs={{0,2},{2,4},{4,6},{6,8},{8,10},{10,12},{12,14},{14,16},{16,18},{18... | collective-permute-start | bytes 221192 | tf_op jit(solution)/shard_map/ppermute | solution.py:16
  27.1 47.5 %collective-permute-start.1 = (f32[2,8,3,384]{3,1,2,0:T(8,128)S(1)}, f32[2,8,3,384]{3,1,2,0:T(8,128)S(1)}, u32[]{:S(2)}, u32[]{:S(2)}) collective-permute-start(f32[2,8,3,384]{3,1,2,0:T(8,128)S(1)} %get-tuple-element.33), channel_id=1, source_target_pairs={{2,0},{4,2},{6,4},{8,6},{10,8},{12,10},{14,12},{16,14},{18,16},{20... | collective-permute-start | bytes 221192 | tf_op jit(solution)/shard_map/ppermute | solution.py:17
  120.7 52.6 %slice-start.3 = ((s8[11796480]{0:T(1024)(128)(4,1)}), s8[4194304]{0:T(1024)(128)(4,1)S(1)}, s32[]{:S(2)}) async-start(s8[11796480]{0:T(1024)(128)(4,1)} %bitcast.41), calls=%async_computation.6 | async-start | bytes 8388608
  120.7 52.6 %slice-start.4 = ((s8[11796480]{0:T(1024)(128)(4,1)}), s8[4194304]{0:T(1024)(128)(4,1)S(1)}, s32[]{:S(2)}) async-start(s8[11796480]{0:T(1024)(128)(4,1)} %bitcast.41), calls=%async_computation.7 | async-start | bytes 8388608
  146.3 27.0 %slice-start.5 = ((s8[11796480]{0:T(1024)(128)(4,1)}), s8[3407872]{0:T(1024)(128)(4,1)S(1)}, s32[]{:S(2)}) async-start(s8[11796480]{0:T(1024)(128)(4,1)} %bitcast.41), calls=%async_computation.8 | async-start | bytes 6815744
  213.3 19.8 %copy-start.3 = (f32[120,8,8,387]{3,1,2,0:T(8,128)}, f32[120,8,8,387]{3,1,2,0:T(8,128)S(1)}, u32[]{:S(2)}) copy-start(f32[120,8,8,387]{3,1,2,0:T(8,128)S(1)} %fusion.8) | copy-start | bytes 35665924
  280.1 103.2 %copy-start.1 = (f32[120,8,8,384]{3,1,2,0:T(8,128)}, f32[120,8,8,384]{3,1,2,0:T(8,128)S(1)}, u32[]{:S(2)}) copy-start(f32[120,8,8,384]{3,1,2,0:T(8,128)S(1)} %fusion.60) | copy-start | bytes 35389444
  284.6 55.2 %collective-permute-start.4 = (f32[120,8,3,384]{3,1,2,0:T(8,128)}, f32[120,8,3,384]{3,1,2,0:T(8,128)S(1)}, u32[]{:S(2)}, u32[]{:S(2)}) collective-permute-start(f32[120,8,3,384]{3,1,2,0:T(8,128)} %get-tuple-element.28), channel_id=1, source_target_pairs={{0,2},{2,4},{4,6},{6,8},{8,10},{10,12},{12,14},{14,16},{16,18},{18... | collective-permute-start | bytes 13271048 | tf_op jit(solution)/shard_map/ppermute | solution.py:16
  332.5 50.7 %collective-permute-start.5 = (f32[120,8,3,384]{3,1,2,0:T(8,128)}, f32[120,8,3,384]{3,1,2,0:T(8,128)S(1)}, u32[]{:S(2)}, u32[]{:S(2)}) collective-permute-start(f32[120,8,3,384]{3,1,2,0:T(8,128)} %get-tuple-element.29), channel_id=1, source_target_pairs={{2,0},{4,2},{6,4},{8,6},{10,8},{12,10},{14,12},{16,14},{18,16},{20... | collective-permute-start | bytes 13271048 | tf_op jit(solution)/shard_map/ppermute | solution.py:17
  420.2 52.6 %slice-start = ((s8[11796480]{0:T(1024)(128)(4,1)}), s8[4194304]{0:T(1024)(128)(4,1)S(1)}, s32[]{:S(2)}) async-start(s8[11796480]{0:T(1024)(128)(4,1)} %bitcast.39), calls=%async_computation.3 | async-start | bytes 8388608
  420.2 52.6 %slice-start.1 = ((s8[11796480]{0:T(1024)(128)(4,1)}), s8[4194304]{0:T(1024)(128)(4,1)S(1)}, s32[]{:S(2)}) async-start(s8[11796480]{0:T(1024)(128)(4,1)} %bitcast.39), calls=%async_computation.4 | async-start | bytes 8388608
  445.8 27.0 %slice-start.2 = ((s8[11796480]{0:T(1024)(128)(4,1)}), s8[3407872]{0:T(1024)(128)(4,1)S(1)}, s32[]{:S(2)}) async-start(s8[11796480]{0:T(1024)(128)(4,1)} %bitcast.39), calls=%async_computation.5 | async-start | bytes 6815744
  511.7 19.8 %copy-start.2 = (f32[120,8,8,387]{3,1,2,0:T(8,128)}, f32[120,8,8,387]{3,1,2,0:T(8,128)S(1)}, u32[]{:S(2)}) copy-start(f32[120,8,8,387]{3,1,2,0:T(8,128)S(1)} %fusion.15) | copy-start | bytes 35665924
  592.7 8.3 copy-start.11
  592.7 8.4 copy-start.9
  592.7 10.8 %copy-start.8 = (f32[8,8,384]{2,1,0:T(8,128)S(1)}, f32[8,8,384]{2,1,0:T(8,128)}, u32[]{:S(2)}) copy-start(f32[8,8,384]{2,1,0:T(8,128)} %param.11) | copy-start | bytes 294916
  592.7 137.2 %all-to-all-start = ((f32[120,8,8,384]{3,1,0,2:T(8,128)}), f32[120,8,8,384]{3,1,0,2:T(8,128)}, u32[]{:S(2)}, u32[]{:S(2)}) async-start(f32[120,8,8,384]{3,1,0,2:T(8,128)} %copy.52), calls=%async_computation | async-start | bytes 23592960 | tf_op jit(solution)/shard_map/all_to_all | solution.py:82
  827.4 11.3 %copy-start.6 = (f32[240,1,4,384]{3,2,0,1:T(4,128)S(1)}, f32[240,1,4,384]{3,2,0,1:T(4,128)}, u32[]{:S(2)}) copy-start(f32[240,1,4,384]{3,2,0,1:T(4,128)} %exp.19) | copy-start | bytes 4423684
  839.5 22.0 %copy-start.4 = (f32[240,8,4,384]{3,2,1,0:T(4,128)}, f32[240,8,4,384]{3,2,1,0:T(4,128)S(1)}, u32[]{:S(2)}) copy-start(f32[240,8,4,384]{3,2,1,0:T(4,128)S(1)} %get-tuple-element.25) | copy-start | bytes 35389444
  861.5 137.5 %all-to-all-start.1 = ((f32[240,8,4,384]{3,2,1,0:T(4,128)}), f32[240,8,4,384]{3,2,1,0:T(4,128)}, u32[]{:S(2)}, u32[]{:S(2)}) async-start(f32[240,8,4,384]{3,2,1,0:T(4,128)} %copy-done.4), calls=%async_computation.1 | async-start | bytes 23592960 | tf_op jit(solution)/shard_map/all_to_all | solution.py:94
  (2 other events, 10.3 us)
where the time goes:
time: 1030 us; the launch traced here: 1020 us
  other arithmetic  412 us (40%)
  waiting for transfers between devices  345 us (33%)
  local copies, waits for them, and re-layouts  146 us (14%)
  starting transfers between devices  79.1 us (8%)
  blocking collectives  21.9 us (2%)
  matrix products  19.3 us (2%)
    all_to_all x1, waiting for transfers between devices, on_device(): lax.all_to_all(column_out, 'spec', split_axis=0, concat_axis=2, tiled=True)  128 us
    all_to_all x1, waiting for transfers between devices, on_device(): lax.all_to_all(field, 'spec', split_axis=2, concat_axis=0, tiled=True)  126 us
    select_n x4, other arithmetic, sweep(): flux = jnp.where(face >= 0.0, upwind, downwind)  120 us
    sub x4, other arithmetic, sweep(): 7.0 / 12.0 * (cut(field, 1, count - 2) + cut(field, 2, count - 1))  105 us
    sub x4, other arithmetic, sweep(): slope = upper - lower  90.9 us
    sub x4, other arithmetic, sweep(): cut(field, 3, count - 3)  61.2 us
    ppermute x3, starting transfers between devices, padded_2(): before = lax.ppermute(last, axis, up)  51.7 us
    ppermute x3, waiting for transfers between devices, padded_2(): before = lax.ppermute(last, axis, up)  45.9 us
  transfers between devices with their start and end apart: 8, of which 6 were waited for; matrix products, arithmetic and copies ran while one was open for 2% of the time, Pallas kernels for 0%

commit v1 on v0

v1 whole, which is shorter than its diff:
```python
import functools

import jax
import jax.numpy as jnp
from jax import lax
from jax.experimental import pallas as pl
from jax.experimental.pallas import tpu as pltpu
from jax.sharding import PartitionSpec as P

HALO = 6


def flux_weights(c):
    a = 0.5 * c
    ab = a * (1.0 - 2.0 * c / 3.0)
    high, low, own = 1.0 - a - 3.0 * ab, a - 3.0 * ab, 6.0 * ab
    up = [
        -low / 12.0,
        (7.0 * low - high) / 12.0,
        7.0 * (low + high) / 12.0 + own,
        (7.0 * high - low) / 12.0,
        -high / 12.0,
        jnp.zeros_like(c),
    ]
    ab = a * (1.0 + 2.0 * c / 3.0)
    low, high, own = 1.0 + a + 3.0 * ab, 3.0 * ab - a, -6.0 * ab
    down = [
        jnp.zeros_like(c),
        -low / 12.0,
        (7.0 * low - high) / 12.0,
        7.0 * (low + high) / 12.0 + own,
        (7.0 * high - low) / 12.0,
        -high / 12.0,
    ]
    return [c * jnp.where(c >= 0.0, u, d) for u, d in zip(up, down)]


def sweep_weights(below, above):
    lo, hi = flux_weights(below), flux_weights(above)
    weights = []
    for k in range(-3, 4):
        w = jnp.ones_like(below) if k == 0 else jnp.zeros_like(below)
        if -2 <= k <= 3:
            w = w - hi[k + 2]
        if -3 <= k <= 2:
            w = w + lo[k + 3]
        weights.append(w)
    return weights


def transport_kernel(group, tracers, before, after, wx, wy, wm, out, ext, mid):
    rows = wm.shape[0]
    lanes = wm.shape[2]

    def rows_of(ref, r):
        acc = wx[0, r[0]] * ref[r[1]]
        for k in range(1, 7):
            acc = acc + wx[k, r[0]] * ref[r[1] + k]
        return acc

    def lanes_of(q, r):
        left = pltpu.roll(q, 1, 1)
        right = pltpu.roll(q, lanes - 1, 1)
        total = wy[3, r] * q + wy[2, r] * left + wy[4, r] * right
        total = total + pltpu.roll(wy[0, r] * q + wy[1, r] * right, 3, 1)
        return total + pltpu.roll(wy[6, r] * q + wy[5, r] * left, lanes - 3, 1)

    def one(s, _):
        ext[0:HALO] = before[s]
        ext[HALO : HALO + rows] = jnp.transpose(tracers[s], (1, 0, 2))
        ext[HALO + rows :] = after[s]
        for r in range(rows + 6):
            mid[r] = lanes_of(rows_of(ext, (r, r)), r)
        for r in range(rows):
            q = lanes_of(rows_of(mid, (r + 3, r)), r + 3)
            share = wm[r]
            mean = jnp.sum(share * q, axis=0, keepdims=True)
            ext[r] = jnp.where(share > 0.0, mean, q)
        out[s] = jnp.transpose(ext[0:rows], (1, 0, 2))
        return 0

    lax.fori_loop(0, group, one, 0)


def transport(chunk, start, tracers, before, after, wx, wy, wm):
    levels, rows, lanes = tracers.shape[1:]
    group = max(g for g in (1, 2, 3, 5, 6) if chunk % g == 0)
    first = start // group

    def whole(array):
        return pl.BlockSpec(array.shape, lambda i: (0,) * array.ndim)

    return pl.pallas_call(
        functools.partial(transport_kernel, group),
        grid=(chunk // group,),
        out_shape=jax.ShapeDtypeStruct((chunk, levels, rows, lanes), jnp.float32),
        in_specs=[
            pl.BlockSpec((group, levels, rows, lanes), lambda i: (i + first, 0, 0, 0)),
            pl.BlockSpec((group, HALO, levels, lanes), lambda i: (i, 0, 0, 0)),
            pl.BlockSpec((group, HALO, levels, lanes), lambda i: (i, 0, 0, 0)),
            whole(wx),
            whole(wy),
            whole(wm),
        ],
        out_specs=pl.BlockSpec((group, levels, rows, lanes), lambda i: (i, 0, 0, 0)),
        scratch_shapes=[
            pltpu.VMEM((rows + 2 * HALO, levels, lanes), jnp.float32),
            pltpu.VMEM((rows + 6, levels, lanes), jnp.float32),
        ],
        compiler_params=pltpu.CompilerParams(vmem_limit_bytes=24 * 1024 * 1024),
        cost_estimate=pl.CostEstimate(
            flops=chunk * levels * (4 * rows + 12) * lanes * 15,
            bytes_accessed=chunk * levels * (2 * rows + 2 * HALO) * lanes * 4,
            transcendentals=0,
        ),
    )(tracers, before, after, wx, wy, wm)


def neighbours(last, leading, axis):
    devices = lax.axis_size(axis)
    up = [(i, i + 1) for i in range(devices - 1)]
    down = [(i + 1, i) for i in range(devices - 1)]
    return lax.ppermute(last, axis, up), lax.ppermute(leading, axis, down)


def on_device(tracers, courant, layer_mass, pbl_top, land_type, rates, coupling):
    species, levels, rows, lanes = tracers.shape
    parts, place = lax.axis_size("spec"), lax.axis_index("spec")
    strips, strip = lax.axis_size("space"), lax.axis_index("space")

    before, after = neighbours(courant[:, :, rows - 3 :], courant[:, :, :4], "space")
    pieces = max(n for n in (1, 2, 3, 4, 5) if species % n == 0)
    chunk = species // pieces
    halos = []
    for piece in range(pieces):
        block = tracers[piece * chunk : (piece + 1) * chunk]
        last, leading = block[:, :, rows - HALO :], block[:, :, :HALO]
        if piece:
            tie = (before, after) if piece == 1 else halos[piece - 2]
            *tie, last, leading = lax.optimization_barrier((*tie, last, leading))
            if piece == 1:
                before, after = tie
            else:
                halos[piece - 2] = tuple(tie)
        halos.append(
            neighbours(
                jnp.transpose(last, (0, 2, 1, 3)),
                jnp.transpose(leading, (0, 2, 1, 3)),
                "space",
            )
        )
    speed = jnp.transpose(jnp.concatenate([before, courant, after], axis=2), (0, 2, 1, 3))
    row = strip * rows + jnp.arange(-3, rows + 3)
    exists = ((row >= 0) & (row < strips * rows))[:, None, None]
    wx = jnp.stack(
        [jnp.where(exists, w, 0.0) for w in sweep_weights(speed[0, :-1], speed[0, 1:])]
    )
    along = speed[1, :-1]
    above = jnp.pad(along[:, :, 1:], ((0, 0), (0, 0), (0, 1)))
    lane = jnp.arange(lanes)
    wy = []
    for k, w in zip(range(-3, 4), sweep_weights(along, above)):
        w = jnp.where((lane + k >= 0) & (lane + k < lanes), w, 0.0)
        wy.append(jnp.roll(w, -3 if k < -1 else 3 if k > 1 else 0, axis=-1))
    wy = jnp.stack(wy)
    inside = jnp.arange(levels, dtype=jnp.int32)[:, None, None] < pbl_top[None]
    share = jnp.where(inside, layer_mass, 0.0)
    wm = jnp.transpose(share / jnp.sum(share, axis=0, keepdims=True), (1, 0, 2))

    mine, theirs = [], [[] for _ in range(parts - 1)]
    for piece in range(pieces):
        mixed = transport(chunk, piece * chunk, tracers, *halos[piece], wx, wy, wm)
        mine.append(mixed)
        for away in range(1, parts):
            theirs[away - 1].append(
                lax.ppermute(mixed, "spec", [(i, (i + away) % parts) for i in range(parts)])
            )

    matrix = lax.dynamic_slice_in_dim(coupling, place * species, species, 0)

    def times_all(away, fields):
        source = lax.rem(place + parts - away, parts)
        part = lax.dynamic_slice_in_dim(matrix, source * species, species, 1)
        field = jnp.concatenate(fields, axis=0)
        return jnp.einsum("ij,jlrx->ilrx", part, field, precision=lax.Precision.HIGH)

    coupled = jnp.concatenate(mine, axis=0) + times_all(0, mine)
    for away in range(1, parts):
        coupled = coupled + times_all(away, theirs[away - 1])

    own_rates = lax.dynamic_slice_in_dim(rates, place * species, species, 1)
    kinds = jnp.arange(rates.shape[0], dtype=jnp.int32)[:, None]
    onehot = (land_type.reshape(1, -1) == kinds).astype(jnp.float32)
    loss = jnp.dot(own_rates.T, onehot, precision=lax.Precision.HIGHEST)
    keep = jnp.exp(-loss.reshape(species, rows, lanes))
    bottom = coupled[:, 0]
    kept = bottom * keep
    level = jnp.arange(levels)[None, :, None, None]
    updated = jnp.where(level == 0, kept[:, None], coupled)
    return updated, (bottom - kept) * layer_mass[0][None]


def solution(mesh):
    return jax.shard_map(
        on_device,
        mesh=mesh,
        in_specs=(
            P("spec", None, "space", None),
            P(None, None, "space", None),
            P(None, "space", None),
            P("space", None),
            P("space", None),
            P(),
            P(),
        ),
        out_specs=(P("spec", None, "space", None), P("spec", "space", None)),
        check_vma=False,
    )
```

time: 1030 us -> 526 us (0.51)
  other arithmetic: 412 us -> 31.7 us
  waiting for transfers between devices: 345 us -> 141 us
  Pallas kernels: 0 us -> 88.6 us
  local copies, waits for them, and re-layouts: 146 us -> 74.7 us
  starting transfers between devices: 79.1 us -> 145 us
  blocking collectives: 21.9 us -> 0 us
  matrix products: 19.3 us -> 35.1 us
    sub x12 -> x0, other arithmetic: 257 us -> none  [the longest x4 105 us: sweep(): 7.0 / 12.0 * (cut(field, 1, count - 2) + cut(field, 2, count - 1))]
    all_to_all x2 -> x0, waiting for transfers between devices: 254 us -> none  [the longest x1 128 us: on_device(): lax.all_to_all(column_out, 'spec', split_axis=0, concat_axis=2, tiled=True)]
    select_n x4 -> x2, other arithmetic: 120 us -> 12.2 us  [the longest x1 11.8 us: on_device(): updated = jnp.where(level == 0, kept[:, None], coupled)]
    pallas_call x0 -> x5, Pallas kernels: none -> 88.6 us  [transport(): pl.pallas_call(functools.partial(transport_kernel, group), grid=(chunk //...]
    ppermute x6 -> x17, starting transfers between devices: 62.7 us -> 145 us  [the longest x12 139 us: neighbours(): return (lax.ppermute(last, axis, up), lax.ppermute(leading, axis, down))]
    all_to_all x5 -> x0, local copies, waits for them, and re-layouts: 55.1 us -> none  [the longest x2 29.8 us: on_device(): lax.all_to_all(field, 'spec', split_axis=2, concat_axis=0, tiled=True)]
    ppermute x6 -> x17, waiting for transfers between devices: 91.3 us -> 141 us  [the longest x5 129 us: on_device(): lax.ppermute(mixed, 'spec', [(i, (i + away) % parts) for i in range(parts)])]
    all_to_all x1 -> x0, blocking collectives: 21.9 us -> none  [on_device(): lax.all_to_all(column_flux[:, None], 'spec', split_axis=0, concat_axis=2,...]
  transfers between devices with their start and end apart: 8 -> 17, of which waited for: 6 -> 7; matrix products, arithmetic and copies ran while one was open for 2% -> 11% of each run, Pallas kernels for 0% -> 17%
where the time goes in v1:
time: 526 us; the launch traced here: 518 us
  starting transfers between devices  145 us (28%)
  waiting for transfers between devices  141 us (27%)
  Pallas kernels  88.6 us (17%)
  local copies, waits for them, and re-layouts  74.7 us (14%)
  matrix products  35.1 us (7%)
  other arithmetic  31.7 us (6%)
    ppermute x12, starting transfers between devices, neighbours(): return (lax.ppermute(last, axis, up), lax.ppermute(leading, axis, down))  139 us
    ppermute x5, waiting for transfers between devices, on_device(): lax.ppermute(mixed, 'spec', [(i, (i + away) % parts) for i in range(parts)])  129 us
    pallas_call x5, Pallas kernels, transport(): pl.pallas_call(functools.partial(transport_kernel, group), grid=(chunk //...  88.6 us
    unnamed x60, local copies, waits for them, and re-layouts  48 us
    dot_general x2, matrix products, times_all(): jnp.einsum('ij,jlrx->ilrx', part, field, precision=lax.Precision.HIGH)  33.1 us
    add x1, other arithmetic, on_device(): coupled = coupled + times_all(away, theirs[away - 1])  14.7 us
    slice x1, local copies, waits for them, and re-layouts, on_device(): last, leading = (block[:, :, rows - HALO:], block[:, :, :HALO])  14 us
    ppermute x12, waiting for transfers between devices, neighbours(): return (lax.ppermute(last, axis, up), lax.ppermute(leading, axis, down))  12.7 us
  transfers between devices with their start and end apart: 17, of which 7 were waited for; matrix products, arithmetic and copies ran while one was open for 11% of the time, Pallas kernels for 17%

profile of v1, /device:TPU:24, one launch (start us, length us, event | category | flops | bytes accessed | tf_op | source)
XLA Modules:
  0.0 517.7 jit_solution(16663112420106317621)
XLA Ops:
  0.6 14.0 %fusion.46 = (f32[24,8,6,384]{3,2,1,0:T(8,128)S(1)}, f32[24,8,6,384]{3,2,1,0:T(8,128)}, f32[24,8,6,384]{3,2,1,0:T(8,128)}, f32[24,8,6,384]{3,2,1,0:T(8,128)}, f3...) fusion(f32[120,8,8,384]{3,2,1,0:T(8,128)} %tracers.9), kind=kLoop, calls=%fused_computation.125 | loop fusion | bytes 35389440 | tf_op jit(solution)/shard_map/slice | solution.py:137
  21.6 4.5 collective-permute-start.1
  28.2 4.5 collective-permute-start.3
  36.0 8.0 %collective-permute-done.2 = f32[2,8,3,384]{3,1,2,0:T(8,128)S(1)} collective-permute-done((f32[2,8,3,384]{3,1,2,0:T(8,128)S(1)}, f32[2,8,3,384]{3,1,2,0:T(8,128)S(1)}, u32[]{:S(2)}, u32[]{:S(2)}) %collective-permute-start.2) | collective-permute-done | bytes 73760 | tf_op jit(solution)/shard_map/ppermute | solution.py:123
  43.9 3.5 collective-permute-done.3
  47.5 37.0 %collective-permute-start.4 = (f32[24,6,8,384]{3,2,1,0:T(8,128)}, f32[24,6,8,384]{3,2,1,0:T(8,128)S(1)}, u32[]{:S(2)}, u32[]{:S(2)}) collective-permute-start(f32[24,6,8,384]{3,2,1,0:T(8,128)} %bitcast.84), channel_id=1, source_target_pairs={{0,2},{2,4},{4,6},{6,8},{8,10},{10,12},{12,14},{14,16},{16,18},{18... | collective-permute-start | bytes 5308424 | tf_op jit(solution)/shard_map/ppermute | solution.py:123
  100.7 4.1 collective-permute-start.7
  106.8 41.6 %collective-permute-start.8 = (f32[24,6,8,384]{3,2,1,0:T(8,128)S(1)}, f32[24,6,8,384]{3,2,1,0:T(8,128)S(1)}, u32[]{:S(2)}, u32[]{:S(2)}) collective-permute-start(f32[24,6,8,384]{3,2,1,0:T(8,128)S(1)} %bitcast.82), channel_id=1, source_target_pairs={{0,2},{2,4},{4,6},{6,8},{8,10},{10,12},{12,14},{14,16},{16,18},{18... | collective-permute-start | bytes 5308424 | tf_op jit(solution)/shard_map/ppermute | solution.py:123
  151.4 34.9 %collective-permute-start.10 = (f32[24,6,8,384]{3,2,1,0:T(8,128)}, f32[24,6,8,384]{3,2,1,0:T(8,128)}, u32[]{:S(2)}, u32[]{:S(2)}) collective-permute-start(f32[24,6,8,384]{3,2,1,0:T(8,128)} %bitcast.18), channel_id=1, source_target_pairs={{0,2},{2,4},{4,6},{6,8},{8,10},{10,12},{12,14},{14,16},{16,18},{18... | collective-permute-start | bytes 5308424 | tf_op jit(solution)/shard_map/ppermute | solution.py:123
  188.8 18.4 %shard_map.86 = f32[24,8,8,384]{3,2,1,0:T(8,128)} custom-call(f32[120,8,8,384]{3,2,1,0:T(8,128)S(1)} %bitcast.79, f32[24,6,8,384]{3,2,1,0:T(8,128)} %collective-permute-done.before, f32[24,6,8,384]{3,2,1,0:T(8,128)} %collective-permute-done.1.after, f32[7,14,8,384]{3,2,1,0:T(8,128)S(1)} %select_dynamic-update-slice_fusion.wx, ...), custom_call_target="tpu_custom_call" | custom-call | flops 48660480 | bytes 8257536 | tf_op jit(solution)/shard_map/pallas_call | solution.py:93
  208.8 17.2 %shard_map.87 = f32[24,8,8,384]{3,2,1,0:T(8,128)} custom-call(f32[120,8,8,384]{3,2,1,0:T(8,128)S(1)} %bitcast.79, f32[24,6,8,384]{3,2,1,0:T(8,128)S(1)} %collective-permute-done.4.before, f32[24,6,8,384]{3,2,1,0:T(8,128)S(1)} %collective-permute-done.5.after, f32[7,14,8,384]{3,2,1,0:T(8,128)S(1)} %select_dynamic-update-slice_fusion.wx, ...), custom_call_target="tpu_custom_call" | custom-call | flops 48660480 | bytes 8257536 | tf_op jit(solution)/shard_map/pallas_call | solution.py:93
  229.8 4.3 copy-done.1
  237.1 17.2 %shard_map.88 = f32[24,8,8,384]{3,2,1,0:T(8,128)} custom-call(f32[120,8,8,384]{3,2,1,0:T(8,128)S(1)} %copy-done.1, f32[24,6,8,384]{3,2,1,0:T(8,128)S(1)} %copy-done.4, f32[24,6,8,384]{3,2,1,0:T(8,128)S(1)} %copy-done.6, f32[7,14,8,384]{3,2,1,0:T(8,128)S(1)} %select_dynamic-update-slice_fusion.wx, f32[7,14,8,384]{3,2,1,0:T(8,128)S(1)} %fusion.12.wy, ...), custom_call_target="tpu_custom_call" | custom-call | flops 48660480 | bytes 8257536 | tf_op jit(solution)/shard_map/pallas_call | solution.py:93
  255.8 18.3 %shard_map.89 = f32[24,8,8,384]{3,2,1,0:T(8,128)} custom-call(f32[120,8,8,384]{3,2,1,0:T(8,128)S(1)} %copy-done.1, f32[24,6,8,384]{3,2,1,0:T(8,128)S(1)} %copy-done.8, f32[24,6,8,384]{3,2,1,0:T(8,128)} %collective-permute-done.9.after, f32[7,14,8,384]{3,2,1,0:T(8,128)S(1)} %select_dynamic-update-slice_fusion.wx, f32[7,14,8,384]{3,2,1,0:T(8,128)S(1)} %fusion.12.wy, ...), custom_call_target="tpu_custom_call" | custom-call | flops 48660480 | bytes 8257536 | tf_op jit(solution)/shard_map/pallas_call | solution.py:93
  277.4 4.3 copy-done.2
  281.8 17.6 %shard_map.90 = f32[24,8,8,384]{3,2,1,0:T(8,128)S(1)} custom-call(f32[120,8,8,384]{3,2,1,0:T(8,128)S(1)} %copy-done.2, f32[24,6,8,384]{3,2,1,0:T(8,128)} %collective-permute-done.10.before, f32[24,6,8,384]{3,2,1,0:T(8,128)} %collective-permute-done.11.after, f32[7,14,8,384]{3,2,1,0:T(8,128)S(1)} %select_dynamic-update-slice_fusion.wx, ...), custom_call_target="tpu_custom_call" | custom-call | flops 48660480 | bytes 8257536 | tf_op jit(solution)/shard_map/pallas_call | solution.py:93
  315.7 13.2 %fusion.3 = f32[120,8,8,384]{3,0,2,1:T(8,128)} fusion(f32[120,8,8,384]{3,2,1,0:T(8,128)S(1)} %constant_dynamic-update-slice_fusion, f32[240,240]{1,0:T(8,128)S(1)} %copy-done, s32[]{:T(128)S(6)} %select_n.200, s32[]{:T(128)S(6)} %select_n.202), kind=kOutput, calls=%fused_computation.5 | convolution fusion | flops 2123366400 | bytes 23654408 | tf_op jit(solution)/shard_map/ij,jlrx->ilrx/dot_general | solution.py:185
  328.9 33.9 %collective-permute-done.14 = f32[24,8,8,384]{3,2,1,0:T(8,128)} collective-permute-done((f32[24,8,8,384]{3,2,1,0:T(8,128)}, f32[24,8,8,384]{3,2,1,0:T(8,128)}, u32[]{:S(2)}, u32[]{:S(2)}) %collective-permute-start.14) | collective-permute-done | bytes 2359328 | tf_op jit(solution)/shard_map/ppermute | solution.py:176
  366.1 47.3 %collective-permute-done.15 = f32[24,8,8,384]{3,2,1,0:T(8,128)} collective-permute-done((f32[24,8,8,384]{3,2,1,0:T(8,128)}, f32[24,8,8,384]{3,2,1,0:T(8,128)}, u32[]{:S(2)}, u32[]{:S(2)}) %collective-permute-start.15) | collective-permute-done | bytes 2359328 | tf_op jit(solution)/shard_map/ppermute | solution.py:176
  416.6 46.8 %collective-permute-done.16 = f32[24,8,8,384]{3,2,1,0:T(8,128)S(1)} collective-permute-done((f32[24,8,8,384]{3,2,1,0:T(8,128)S(1)}, f32[24,8,8,384]{3,2,1,0:T(8,128)S(1)}, u32[]{:S(2)}, u32[]{:S(2)}) %collective-permute-start.16) | collective-permute-done | bytes 2359328 | tf_op jit(solution)/shard_map/ppermute | solution.py:176
  465.0 19.9 %fusion.1 = f32[120,8,8,384]{3,0,2,1:T(8,128)} fusion(f32[120,8,8,384]{3,2,1,0:T(8,128)} %constant_dynamic-update-slice_fusion.5, f32[240,240]{1,0:T(8,128)S(1)} %copy-done, s32[]{:T(128)S(6)} %select_n.200, s32[]{:T(128)S(6)} %select_n.204), kind=kOutput, calls=%fused_computation.2 | convolution fusion | flops 2123366400 | bytes 23654408 | tf_op jit(solution)/shard_map/ij,jlrx->ilrx/dot_general | solution.py:185
  484.9 14.7 %copy_add_fusion = f32[120,8,8,384]{3,2,1,0:T(8,128)S(1)} fusion(f32[120,8,8,384]{3,0,2,1:T(8,128)} %fusion.1, f32[120,8,8,384]{3,2,1,0:T(8,128)S(1)} %constant_dynamic-update-slice_fusion, f32[120,8,8,384]{3,0,2,1:T(8,128)} %fusion.3), kind=kLoop, calls=%fused_computation.1 | loop fusion | flops 5898240 | bytes 47185920 | tf_op jit(solution)/shard_map/add | solution.py:189
  499.9 4.3 copy-done.9
  505.5 11.8 %broadcast_select_fusion = f32[120,8,8,384]{3,2,1,0:T(8,128)} fusion(f32[120,8,8,384]{3,2,1,0:T(8,128)} %copy-done.9, f32[120,8,384]{2,1,0:T(8,128)S(1)} %multiply_bitcast_fusion, pred[8]{0:T(512)(128)(4,1)S(1)} %iota_compare_fusion.4), kind=kLoop, calls=%fused_computation.7 | loop fusion | flops 2949120 | bytes 25067528 | tf_op jit(solution)/shard_map/jit(_where)/select_n | solution.py:199
  (129 shorter events, 74.8 us)
Async XLA Ops:
  0.6 315.1 %copy-start = (f32[240,240]{1,0:T(8,128)S(1)}, f32[240,240]{1,0:T(8,128)}, u32[]{:S(2)}) copy-start(f32[240,240]{1,0:T(8,128)} %param.13) | copy-start | bytes 691204
  18.0 80.2 %collective-permute-start = (f32[24,6,8,384]{3,2,1,0:T(8,128)}, f32[24,6,8,384]{3,2,1,0:T(8,128)}, u32[]{:S(2)}, u32[]{:S(2)}) collective-permute-start(f32[24,6,8,384]{3,2,1,0:T(8,128)} %bitcast.75), channel_id=1, source_target_pairs={{0,2},{2,4},{4,6},{6,8},{8,10},{10,12},{12,14},{14,16},{16,18},{18... | collective-permute-start | bytes 5308424 | tf_op jit(solution)/shard_map/ppermute | solution.py:123
  21.6 76.5 %collective-permute-start.1 = (f32[24,6,8,384]{3,2,1,0:T(8,128)}, f32[24,6,8,384]{3,2,1,0:T(8,128)}, u32[]{:S(2)}, u32[]{:S(2)}) collective-permute-start(f32[24,6,8,384]{3,2,1,0:T(8,128)} %bitcast.74), channel_id=1, source_target_pairs={{2,0},{4,2},{6,4},{8,6},{10,8},{12,10},{14,12},{16,14},{18,16},{20... | collective-permute-start | bytes 5308424 | tf_op jit(solution)/shard_map/ppermute | solution.py:123
  26.2 17.7 %collective-permute-start.2 = (f32[2,8,3,384]{3,1,2,0:T(8,128)S(1)}, f32[2,8,3,384]{3,1,2,0:T(8,128)S(1)}, u32[]{:S(2)}, u32[]{:S(2)}) collective-permute-start(f32[2,8,3,384]{3,1,2,0:T(8,128)S(1)} %slice.123), channel_id=1, source_target_pairs={{0,2},{2,4},{4,6},{6,8},{8,10},{10,12},{12,14},{14,16},{16,18},{18... | collective-permute-start | bytes 221192 | tf_op jit(solution)/shard_map/ppermute | solution.py:123
  28.2 19.3 %collective-permute-start.3 = (f32[2,8,4,384]{3,1,2,0:T(8,128)S(1)}, f32[2,8,4,384]{3,1,2,0:T(8,128)S(1)}, u32[]{:S(2)}, u32[]{:S(2)}) collective-permute-start(f32[2,8,4,384]{3,1,2,0:T(8,128)S(1)} %slice.124), channel_id=1, source_target_pairs={{2,0},{4,2},{6,4},{8,6},{10,8},{12,10},{14,12},{16,14},{18,16},{20... | collective-permute-start | bytes 294920 | tf_op jit(solution)/shard_map/ppermute | solution.py:123
  35.9 52.6 %copy-start.14 = (f32[24,8,6,384]{3,2,1,0:T(8,128)S(1)}, f32[24,8,6,384]{3,2,1,0:T(8,128)}, u32[]{:S(2)}) copy-start(f32[24,8,6,384]{3,2,1,0:T(8,128)} %get-tuple-element.44) | copy-start | bytes 5308420
  47.5 58.2 %collective-permute-start.4 = (f32[24,6,8,384]{3,2,1,0:T(8,128)}, f32[24,6,8,384]{3,2,1,0:T(8,128)S(1)}, u32[]{:S(2)}, u32[]{:S(2)}) collective-permute-start(f32[24,6,8,384]{3,2,1,0:T(8,128)} %bitcast.84), channel_id=1, source_target_pairs={{0,2},{2,4},{4,6},{6,8},{8,10},{10,12},{12,14},{14,16},{16,18},{18... | collective-permute-start | bytes 5308424 | tf_op jit(solution)/shard_map/ppermute | solution.py:123
  84.5 22.3 %collective-permute-start.5 = (f32[24,6,8,384]{3,2,1,0:T(8,128)}, f32[24,6,8,384]{3,2,1,0:T(8,128)S(1)}, u32[]{:S(2)}, u32[]{:S(2)}) collective-permute-start(f32[24,6,8,384]{3,2,1,0:T(8,128)} %bitcast.83), channel_id=1, source_target_pairs={{2,0},{4,2},{6,4},{8,6},{10,8},{12,10},{14,12},{16,14},{18,16},{20... | collective-permute-start | bytes 5308424 | tf_op jit(solution)/shard_map/ppermute | solution.py:123
  90.9 97.8 %slice-start = ((s8[11796480]{0:T(1024)(128)(4,1)}), s8[4194304]{0:T(1024)(128)(4,1)S(1)}, s32[]{:S(2)}) async-start(s8[11796480]{0:T(1024)(128)(4,1)} %bitcast.78), calls=%async_computation | async-start | bytes 8388608
  92.5 96.3 %slice-start.1 = ((s8[11796480]{0:T(1024)(128)(4,1)}), s8[4194304]{0:T(1024)(128)(4,1)S(1)}, s32[]{:S(2)}) async-start(s8[11796480]{0:T(1024)(128)(4,1)} %bitcast.78), calls=%async_computation.1 | async-start | bytes 8388608
  97.5 91.3 %slice-start.2 = ((s8[11796480]{0:T(1024)(128)(4,1)}), s8[3407872]{0:T(1024)(128)(4,1)S(1)}, s32[]{:S(2)}) async-start(s8[11796480]{0:T(1024)(128)(4,1)} %bitcast.78), calls=%async_computation.2 | async-start | bytes 6815744
  98.2 53.3 %collective-permute-start.6 = (f32[24,6,8,384]{3,2,1,0:T(8,128)S(1)}, f32[24,6,8,384]{3,2,1,0:T(8,128)S(1)}, u32[]{:S(2)}, u32[]{:S(2)}) collective-permute-start(f32[24,6,8,384]{3,2,1,0:T(8,128)S(1)} %bitcast.86), channel_id=1, source_target_pairs={{0,2},{2,4},{4,6},{6,8},{8,10},{10,12},{12,14},{14,16},{16,18},{18... | collective-permute-start | bytes 5308424 | tf_op jit(solution)/shard_map/ppermute | solution.py:123
  100.7 50.7 %collective-permute-start.7 = (f32[24,6,8,384]{3,2,1,0:T(8,128)S(1)}, f32[24,6,8,384]{3,2,1,0:T(8,128)S(1)}, u32[]{:S(2)}, u32[]{:S(2)}) collective-permute-start(f32[24,6,8,384]{3,2,1,0:T(8,128)S(1)} %bitcast.85), channel_id=1, source_target_pairs={{2,0},{4,2},{6,4},{8,6},{10,8},{12,10},{14,12},{16,14},{18,16},{20... | collective-permute-start | bytes 5308424 | tf_op jit(solution)/shard_map/ppermute | solution.py:123
  106.8 119.2 %collective-permute-start.8 = (f32[24,6,8,384]{3,2,1,0:T(8,128)S(1)}, f32[24,6,8,384]{3,2,1,0:T(8,128)S(1)}, u32[]{:S(2)}, u32[]{:S(2)}) collective-permute-start(f32[24,6,8,384]{3,2,1,0:T(8,128)S(1)} %bitcast.82), channel_id=1, source_target_pairs={{0,2},{2,4},{4,6},{6,8},{8,10},{10,12},{12,14},{14,16},{16,18},{18... | collective-permute-start | bytes 5308424 | tf_op jit(solution)/shard_map/ppermute | solution.py:123
  149.5 104.8 %collective-permute-start.9 = (f32[24,6,8,384]{3,2,1,0:T(8,128)}, f32[24,6,8,384]{3,2,1,0:T(8,128)}, u32[]{:S(2)}, u32[]{:S(2)}) collective-permute-start(f32[24,6,8,384]{3,2,1,0:T(8,128)} %bitcast.17), channel_id=1, source_target_pairs={{2,0},{4,2},{6,4},{8,6},{10,8},{12,10},{14,12},{16,14},{18,16},{20... | collective-permute-start | bytes 5308424 | tf_op jit(solution)/shard_map/ppermute | solution.py:123
  151.4 55.8 %copy-start.3 = (f32[24,6,8,384]{3,2,1,0:T(8,128)}, f32[24,6,8,384]{3,2,1,0:T(8,128)S(1)}, u32[]{:S(2)}) copy-start(f32[24,6,8,384]{3,2,1,0:T(8,128)S(1)} %collective-permute-done.6.before) | copy-start | bytes 5308420
  151.4 55.8 %copy-start.5 = (f32[24,6,8,384]{3,2,1,0:T(8,128)}, f32[24,6,8,384]{3,2,1,0:T(8,128)S(1)}, u32[]{:S(2)}) copy-start(f32[24,6,8,384]{3,2,1,0:T(8,128)S(1)} %collective-permute-done.7.after) | copy-start | bytes 5308420
  151.4 122.6 %collective-permute-start.10 = (f32[24,6,8,384]{3,2,1,0:T(8,128)}, f32[24,6,8,384]{3,2,1,0:T(8,128)}, u32[]{:S(2)}, u32[]{:S(2)}) collective-permute-start(f32[24,6,8,384]{3,2,1,0:T(8,128)} %bitcast.18), channel_id=1, source_target_pairs={{0,2},{2,4},{4,6},{6,8},{8,10},{10,12},{12,14},{14,16},{16,18},{18... | collective-permute-start | bytes 5308424 | tf_op jit(solution)/shard_map/ppermute | solution.py:123
  186.6 90.8 %collective-permute-start.11 = (f32[24,6,8,384]{3,2,1,0:T(8,128)}, f32[24,6,8,384]{3,2,1,0:T(8,128)}, u32[]{:S(2)}, u32[]{:S(2)}) collective-permute-start(f32[24,6,8,384]{3,2,1,0:T(8,128)} %bitcast.19), channel_id=1, source_target_pairs={{2,0},{4,2},{6,4},{8,6},{10,8},{12,10},{14,12},{16,14},{18,16},{20... | collective-permute-start | bytes 5308424 | tf_op jit(solution)/shard_map/ppermute | solution.py:123
  207.2 101.0 %collective-permute-start.12 = (f32[24,8,8,384]{3,2,1,0:T(8,128)}, f32[24,8,8,384]{3,2,1,0:T(8,128)}, u32[]{:S(2)}, u32[]{:S(2)}) collective-permute-start(f32[24,8,8,384]{3,2,1,0:T(8,128)} %shard_map.86), channel_id=1, source_target_pairs={{0,1},{1,0},{2,3},{3,2},{4,5},{5,4},{6,7},{7,6},{8,9},{9,8},{10,11... | collective-permute-start | bytes 7077896 | tf_op jit(solution)/shard_map/ppermute | solution.py:176
  227.3 85.0 %collective-permute-start.13 = (f32[24,8,8,384]{3,2,1,0:T(8,128)}, f32[24,8,8,384]{3,2,1,0:T(8,128)}, u32[]{:S(2)}, u32[]{:S(2)}) collective-permute-start(f32[24,8,8,384]{3,2,1,0:T(8,128)} %shard_map.87), channel_id=1, source_target_pairs={{0,1},{1,0},{2,3},{3,2},{4,5},{5,4},{6,7},{7,6},{8,9},{9,8},{10,11... | collective-permute-start | bytes 7077896 | tf_op jit(solution)/shard_map/ppermute | solution.py:176
  254.3 108.5 %collective-permute-start.14 = (f32[24,8,8,384]{3,2,1,0:T(8,128)}, f32[24,8,8,384]{3,2,1,0:T(8,128)}, u32[]{:S(2)}, u32[]{:S(2)}) collective-permute-start(f32[24,8,8,384]{3,2,1,0:T(8,128)} %shard_map.88), channel_id=1, source_target_pairs={{0,1},{1,0},{2,3},{3,2},{4,5},{5,4},{6,7},{7,6},{8,9},{9,8},{10,11... | collective-permute-start | bytes 7077896 | tf_op jit(solution)/shard_map/ppermute | solution.py:176
  274.1 139.3 %collective-permute-start.15 = (f32[24,8,8,384]{3,2,1,0:T(8,128)}, f32[24,8,8,384]{3,2,1,0:T(8,128)}, u32[]{:S(2)}, u32[]{:S(2)}) collective-permute-start(f32[24,8,8,384]{3,2,1,0:T(8,128)} %shard_map.89), channel_id=1, source_target_pairs={{0,1},{1,0},{2,3},{3,2},{4,5},{5,4},{6,7},{7,6},{8,9},{9,8},{10,11... | collective-permute-start | bytes 7077896 | tf_op jit(solution)/shard_map/ppermute | solution.py:176
  299.3 164.1 %collective-permute-start.16 = (f32[24,8,8,384]{3,2,1,0:T(8,128)S(1)}, f32[24,8,8,384]{3,2,1,0:T(8,128)S(1)}, u32[]{:S(2)}, u32[]{:S(2)}) collective-permute-start(f32[24,8,8,384]{3,2,1,0:T(8,128)S(1)} %shard_map.90), channel_id=1, source_target_pairs={{0,1},{1,0},{2,3},{3,2},{4,5},{5,4},{6,7},{7,6},{8,9},{9,8},{10,11... | collective-permute-start | bytes 7077896 | tf_op jit(solution)/shard_map/ppermute | solution.py:176
  (17 other events, 115.9 us)

commit v2 on v1

--- a/solution.py
+++ b/solution.py
@@ -131,24 +131,19 @@
     before, after = neighbours(courant[:, :, rows - 3 :], courant[:, :, :4], "space")
     pieces = max(n for n in (1, 2, 3, 4, 5) if species % n == 0)
     chunk = species // pieces
-    halos = []
-    for piece in range(pieces):
-        block = tracers[piece * chunk : (piece + 1) * chunk]
-        last, leading = block[:, :, rows - HALO :], block[:, :, :HALO]
-        if piece:
-            tie = (before, after) if piece == 1 else halos[piece - 2]
-            *tie, last, leading = lax.optimization_barrier((*tie, last, leading))
-            if piece == 1:
-                before, after = tie
-            else:
-                halos[piece - 2] = tuple(tie)
-        halos.append(
-            neighbours(
-                jnp.transpose(last, (0, 2, 1, 3)),
-                jnp.transpose(leading, (0, 2, 1, 3)),
-                "space",
-            )
+
+    def halo(field, piece):
+        block = field[piece * chunk : (piece + 1) * chunk]
+        return neighbours(
+            jnp.transpose(block[:, :, rows - HALO :], (0, 2, 1, 3)),
+            jnp.transpose(block[:, :, :HALO], (0, 2, 1, 3)),
+            "space",
         )
+
+    halos = [halo(tracers, 0)]
+    if pieces > 1:
+        before, after, field = lax.optimization_barrier((before, after, tracers))
+        halos.append(halo(field, 1))
     speed = jnp.transpose(jnp.concatenate([before, courant, after], axis=2), (0, 2, 1, 3))
     row = strip * rows + jnp.arange(-3, rows + 3)
     exists = ((row >= 0) & (row < strips * rows))[:, None, None]
@@ -175,6 +170,9 @@
             theirs[away - 1].append(
                 lax.ppermute(mixed, "spec", [(i, (i + away) % parts) for i in range(parts)])
             )
+        if piece + 2 < pieces:
+            mine[piece], field = lax.optimization_barrier((mixed, field))
+            halos.append(halo(field, piece + 2))
 
     matrix = lax.dynamic_slice_in_dim(coupling, place * species, species, 0)
 

time: 526 us -> 528 us (level)
  the two profiles are of different devices: /device:TPU:24 before, /device:TPU:0 now
where the time goes in v2:
time: 528 us; the launch traced here: 518 us
  waiting for transfers between devices  167 us (32%)
  local copies, waits for them, and re-layouts  118 us (22%)
  Pallas kernels  90 us (17%)
  starting transfers between devices  69.1 us (13%)
  other arithmetic  37.5 us (7%)
  matrix products  35.1 us (7%)
    ppermute x5, waiting for transfers between devices, on_device(): lax.ppermute(mixed, 'spec', [(i, (i + away) % parts) for i in range(parts)])  165 us
    pallas_call x5, Pallas kernels, transport(): pl.pallas_call(functools.partial(transport_kernel, group), grid=(chunk //...  90 us
    ppermute x12, starting transfers between devices, neighbours(): return (lax.ppermute(last, axis, up), lax.ppermute(leading, axis, down))  63.4 us
    unnamed x60, local copies, waits for them, and re-layouts  47.4 us
    optimization_barrier x3, local copies, waits for them, and re-layouts, on_device(): mine[piece], field = lax.optimization_barrier((mixed, field))  35 us
    dot_general x2, matrix products, times_all(): jnp.einsum('ij,jlrx->ilrx', part, field, precision=lax.Precision.HIGH)  33.1 us
    add x1, other arithmetic, on_device(): coupled = coupled + times_all(away, theirs[away - 1])  17.7 us
    transpose x4, local copies, waits for them, and re-layouts, halo(): jnp.transpose(block[:, :, :HALO], (0, 2, 1, 3))  16.6 us
  transfers between devices with their start and end apart: 17, of which 5 were waited for; matrix products, arithmetic and copies ran while one was open for 21% of the time, Pallas kernels for 17%

profile of v2, /device:TPU:0, one launch (start us, length us, event | category | flops | bytes accessed | tf_op | source)
XLA Modules:
  0.0 518.2 jit_solution(16105256105451540625)
XLA Ops:
  22.5 11.9 %copy.15 = f32[120,8,8,384]{3,1,2,0:T(8,128)} copy(f32[120,8,8,384]{3,2,1,0:T(8,128)} %tracers.9) | data formatting | bytes 23592960 | tf_op jit(solution)/shard_map/optimization_barrier | solution.py:145
  34.4 4.3 slice_bitcast_fusion.6
  38.6 33.8 %collective-permute-start.4 = (f32[24,6,8,384]{3,2,1,0:T(8,128)}, f32[24,6,8,384]{3,2,1,0:T(8,128)}, u32[]{:S(2)}, u32[]{:S(2)}) collective-permute-start(f32[24,6,8,384]{3,2,1,0:T(8,128)} %get-tuple-element.31), channel_id=1, source_target_pairs={{0,2},{2,4},{4,6},{6,8},{8,10},{10,12},{12,14},{14,16},{16,18},{18... | collective-permute-start | bytes 5308424 | tf_op jit(solution)/shard_map/ppermute | solution.py:123
  76.8 18.6 %shard_map.86 = f32[24,8,8,384]{3,2,1,0:T(8,128)} custom-call(f32[120,8,8,384]{3,2,1,0:T(8,128)S(1)} %bitcast.87, f32[24,6,8,384]{3,2,1,0:T(8,128)} %collective-permute-done.before, f32[24,6,8,384]{3,2,1,0:T(8,128)} %collective-permute-done.1.after, f32[7,14,8,384]{3,2,1,0:T(8,128)S(1)} %select_dynamic-update-slice_fusion.wx, ...), custom_call_target="tpu_custom_call" | custom-call | flops 48660480 | bytes 8257536 | tf_op jit(solution)/shard_map/pallas_call | solution.py:93
  95.4 11.7 %copy.17 = f32[120,8,8,384]{3,1,2,0:T(8,128)} copy(f32[120,8,8,384]{3,2,1,0:T(8,128)} %tracers.9) | data formatting | bytes 23592960 | tf_op jit(solution)/shard_map/optimization_barrier | solution.py:174
  116.6 4.3 copy-done.1
  120.9 18.6 %shard_map.87 = f32[24,8,8,384]{3,2,1,0:T(8,128)} custom-call(f32[120,8,8,384]{3,2,1,0:T(8,128)S(1)} %copy-done.1, f32[24,6,8,384]{3,2,1,0:T(8,128)} %collective-permute-done.4.before, f32[24,6,8,384]{3,2,1,0:T(8,128)} %collective-permute-done.5.after, f32[7,14,8,384]{3,2,1,0:T(8,128)S(1)} %select_dynamic-update-slice_fusion.wx, ...), custom_call_target="tpu_custom_call" | custom-call | flops 48660480 | bytes 8257536 | tf_op jit(solution)/shard_map/pallas_call | solution.py:93
  139.5 11.7 %copy.19 = f32[120,8,8,384]{3,1,2,0:T(8,128)} copy(f32[120,8,8,384]{3,2,1,0:T(8,128)} %tracers.9) | data formatting | bytes 23592960 | tf_op jit(solution)/shard_map/optimization_barrier | solution.py:174
  161.0 4.3 copy-done.2
  165.3 16.6 %shard_map.88 = f32[24,8,8,384]{3,2,1,0:T(8,128)S(1)} custom-call(f32[120,8,8,384]{3,2,1,0:T(8,128)S(1)} %copy-done.2, f32[24,6,8,384]{3,2,1,0:T(8,128)S(1)} %collective-permute-done.6.before, f32[24,6,8,384]{3,2,1,0:T(8,128)S(1)} %collective-permute-done.7.after, f32[7,14,8,384]{3,2,1,0:T(8,128)S(1)} %select_dynamic-update-slice_fusion.wx, ...), custom_call_target="tpu_custom_call" | custom-call | flops 48660480 | bytes 8257536 | tf_op jit(solution)/shard_map/pallas_call | solution.py:93
  183.3 11.7 %copy.21 = f32[120,8,8,384]{3,1,2,0:T(8,128)} copy(f32[120,8,8,384]{3,2,1,0:T(8,128)} %tracers.9) | data formatting | bytes 23592960 | tf_op jit(solution)/shard_map/optimization_barrier | solution.py:174
  199.1 5.5 %collective-permute-start.10 = (f32[24,6,8,384]{3,2,1,0:T(8,128)}, f32[24,6,8,384]{3,2,1,0:T(8,128)}, u32[]{:S(2)}, u32[]{:S(2)}) collective-permute-start(f32[24,6,8,384]{3,2,1,0:T(8,128)} %get-tuple-element.25), channel_id=1, source_target_pairs={{0,2},{2,4},{4,6},{6,8},{8,10},{10,12},{12,14},{14,16},{16,18},{18... | collective-permute-start | bytes 5308424 | tf_op jit(solution)/shard_map/ppermute | solution.py:123
  213.1 4.3 copy-done.3
  218.9 18.4 %shard_map.89 = f32[24,8,8,384]{3,2,1,0:T(8,128)} custom-call(f32[120,8,8,384]{3,2,1,0:T(8,128)S(1)} %copy-done.3, f32[24,6,8,384]{3,2,1,0:T(8,128)S(1)} %copy-done.10, f32[24,6,8,384]{3,2,1,0:T(8,128)} %collective-permute-done.9.after, f32[7,14,8,384]{3,2,1,0:T(8,128)S(1)} %select_dynamic-update-slice_fusion.wx, f32[7,14,8,384]{3,2,1,0:T(8,128)S(1)} %copy-done.6, ...), custom_call_target="tpu_custom_call" | custom-call | flops 48660480 | bytes 8257536 | tf_op jit(solution)/shard_map/pallas_call | solution.py:93
  241.3 4.3 copy-done.4
  245.6 17.8 %shard_map.90 = f32[24,8,8,384]{3,2,1,0:T(8,128)S(1)} custom-call(f32[120,8,8,384]{3,2,1,0:T(8,128)S(1)} %copy-done.4, f32[24,6,8,384]{3,2,1,0:T(8,128)} %collective-permute-done.10.before, f32[24,6,8,384]{3,2,1,0:T(8,128)} %collective-permute-done.11.after, f32[7,14,8,384]{3,2,1,0:T(8,128)S(1)} %select_dynamic-update-slice_fusion.wx, ...), custom_call_target="tpu_custom_call" | custom-call | flops 48660480 | bytes 8257536 | tf_op jit(solution)/shard_map/pallas_call | solution.py:93
  274.6 36.5 %collective-permute-done.13 = f32[24,8,8,384]{3,2,1,0:T(8,128)} collective-permute-done((f32[24,8,8,384]{3,2,1,0:T(8,128)}, f32[24,8,8,384]{3,2,1,0:T(8,128)}, u32[]{:S(2)}, u32[]{:S(2)}) %collective-permute-start.13) | collective-permute-done | bytes 2359328 | tf_op jit(solution)/shard_map/ppermute | solution.py:171
  314.7 13.1 %fusion.3 = f32[120,8,8,384]{3,0,2,1:T(8,128)} fusion(f32[120,8,8,384]{3,2,1,0:T(8,128)S(1)} %constant_dynamic-update-slice_fusion, f32[240,240]{1,0:T(8,128)S(1)} %copy-done, s32[]{:T(128)S(6)} %select_n.200, s32[]{:T(128)S(6)} %select_n.202), kind=kOutput, calls=%fused_computation.5 | convolution fusion | flops 2123366400 | bytes 23654408 | tf_op jit(solution)/shard_map/ij,jlrx->ilrx/dot_general | solution.py:183
  327.8 33.9 %collective-permute-done.14 = f32[24,8,8,384]{3,2,1,0:T(8,128)} collective-permute-done((f32[24,8,8,384]{3,2,1,0:T(8,128)}, f32[24,8,8,384]{3,2,1,0:T(8,128)}, u32[]{:S(2)}, u32[]{:S(2)}) %collective-permute-start.14) | collective-permute-done | bytes 2359328 | tf_op jit(solution)/shard_map/ppermute | solution.py:171
  365.0 47.3 %collective-permute-done.15 = f32[24,8,8,384]{3,2,1,0:T(8,128)} collective-permute-done((f32[24,8,8,384]{3,2,1,0:T(8,128)}, f32[24,8,8,384]{3,2,1,0:T(8,128)}, u32[]{:S(2)}, u32[]{:S(2)}) %collective-permute-start.15) | collective-permute-done | bytes 2359328 | tf_op jit(solution)/shard_map/ppermute | solution.py:171
  415.5 47.2 %collective-permute-done.16 = f32[24,8,8,384]{3,2,1,0:T(8,128)S(1)} collective-permute-done((f32[24,8,8,384]{3,2,1,0:T(8,128)S(1)}, f32[24,8,8,384]{3,2,1,0:T(8,128)S(1)}, u32[]{:S(2)}, u32[]{:S(2)}) %collective-permute-start.16) | collective-permute-done | bytes 2359328 | tf_op jit(solution)/shard_map/ppermute | solution.py:171
  464.3 19.9 %fusion.1 = f32[120,8,8,384]{3,0,2,1:T(8,128)} fusion(f32[120,8,8,384]{3,2,1,0:T(8,128)} %constant_dynamic-update-slice_fusion.5, f32[240,240]{1,0:T(8,128)S(1)} %copy-done, s32[]{:T(128)S(6)} %select_n.200, s32[]{:T(128)S(6)} %select_n.204), kind=kOutput, calls=%fused_computation.2 | convolution fusion | flops 2123366400 | bytes 23654408 | tf_op jit(solution)/shard_map/ij,jlrx->ilrx/dot_general | solution.py:183
  484.2 17.7 %copy_add_fusion = f32[120,8,8,384]{3,2,1,0:T(8,128)} fusion(f32[120,8,8,384]{3,0,2,1:T(8,128)} %fusion.1, f32[120,8,8,384]{3,2,1,0:T(8,128)S(1)} %constant_dynamic-update-slice_fusion, f32[120,8,8,384]{3,0,2,1:T(8,128)} %fusion.3), kind=kLoop, calls=%fused_computation.1 | loop fusion | flops 5898240 | bytes 47185920 | tf_op jit(solution)/shard_map/add | solution.py:187
  506.2 11.8 %broadcast_select_fusion = f32[120,8,8,384]{3,2,1,0:T(8,128)} fusion(f32[120,8,8,384]{3,2,1,0:T(8,128)} %copy_add_fusion, f32[120,8,384]{2,1,0:T(8,128)S(1)} %multiply_bitcast_fusion, pred[8]{0:T(512)(128)(4,1)S(1)} %iota_compare_fusion.4), kind=kLoop, calls=%fused_computation.7 | loop fusion | flops 2949120 | bytes 25067528 | tf_op jit(solution)/shard_map/jit(_where)/select_n | solution.py:197
  (129 shorter events, 91.7 us)
Async XLA Ops:
  0.6 314.0 %copy-start = (f32[240,240]{1,0:T(8,128)S(1)}, f32[240,240]{1,0:T(8,128)}, u32[]{:S(2)}) copy-start(f32[240,240]{1,0:T(8,128)} %param.13) | copy-start | bytes 691204
  5.3 71.0 %collective-permute-start = (f32[24,6,8,384]{3,2,1,0:T(8,128)}, f32[24,6,8,384]{3,2,1,0:T(8,128)}, u32[]{:S(2)}, u32[]{:S(2)}) collective-permute-start(f32[24,6,8,384]{3,2,1,0:T(8,128)} %bitcast.83), channel_id=1, source_target_pairs={{0,2},{2,4},{4,6},{6,8},{8,10},{10,12},{12,14},{14,16},{16,18},{18... | collective-permute-start | bytes 5308424 | tf_op jit(solution)/shard_map/ppermute | solution.py:123
  10.5 65.8 %collective-permute-start.1 = (f32[24,6,8,384]{3,2,1,0:T(8,128)}, f32[24,6,8,384]{3,2,1,0:T(8,128)}, u32[]{:S(2)}, u32[]{:S(2)}) collective-permute-start(f32[24,6,8,384]{3,2,1,0:T(8,128)} %bitcast.82), channel_id=1, source_target_pairs={{2,0},{4,2},{6,4},{8,6},{10,8},{12,10},{14,12},{16,14},{18,16},{20... | collective-permute-start | bytes 5308424 | tf_op jit(solution)/shard_map/ppermute | solution.py:123
  11.9 6.2 %collective-permute-start.2 = (f32[2,8,3,384]{3,1,2,0:T(8,128)S(1)}, f32[2,8,3,384]{3,1,2,0:T(8,128)S(1)}, u32[]{:S(2)}, u32[]{:S(2)}) collective-permute-start(f32[2,8,3,384]{3,1,2,0:T(8,128)S(1)} %slice.123), channel_id=1, source_target_pairs={{0,2},{2,4},{4,6},{6,8},{8,10},{10,12},{12,14},{14,16},{16,18},{18... | collective-permute-start | bytes 221192 | tf_op jit(solution)/shard_map/ppermute | solution.py:123
  15.9 4.4 collective-permute-start.3
  22.5 54.3 %slice-start = ((s8[11796480]{0:T(1024)(128)(4,1)}), s8[3407872]{0:T(1024)(128)(4,1)S(1)}, s32[]{:S(2)}) async-start(s8[11796480]{0:T(1024)(128)(4,1)} %bitcast.86), calls=%async_computation | async-start | bytes 6815744
  22.5 54.3 %slice-start.1 = ((s8[11796480]{0:T(1024)(128)(4,1)}), s8[4194304]{0:T(1024)(128)(4,1)S(1)}, s32[]{:S(2)}) async-start(s8[11796480]{0:T(1024)(128)(4,1)} %bitcast.86), calls=%async_computation.1 | async-start | bytes 8388608
  34.4 42.4 %slice-start.2 = ((s8[11796480]{0:T(1024)(128)(4,1)}), s8[4194304]{0:T(1024)(128)(4,1)S(1)}, s32[]{:S(2)}) async-start(s8[11796480]{0:T(1024)(128)(4,1)} %bitcast.86), calls=%async_computation.2 | async-start | bytes 8388608
  38.6 36.2 %copy-start.13 = (f32[14,8,384]{2,1,0:T(8,128)S(1)}, f32[14,8,384]{2,1,0:T(8,128)}, u32[]{:S(2)}) copy-start(f32[14,8,384]{2,1,0:T(8,128)} %copy-done.12) | copy-start | bytes 516100
  38.6 36.3 %copy-start.15 = (f32[14,8,3]{2,1,0:T(8,128)S(1)}, f32[14,8,3]{2,1,0:T(8,128)}, u32[]{:S(2)}) copy-start(f32[14,8,3]{2,1,0:T(8,128)} %slice.133) | copy-start | bytes 4036
  38.6 77.9 %collective-permute-start.4 = (f32[24,6,8,384]{3,2,1,0:T(8,128)}, f32[24,6,8,384]{3,2,1,0:T(8,128)}, u32[]{:S(2)}, u32[]{:S(2)}) collective-permute-start(f32[24,6,8,384]{3,2,1,0:T(8,128)} %get-tuple-element.31), channel_id=1, source_target_pairs={{0,2},{2,4},{4,6},{6,8},{8,10},{10,12},{12,14},{14,16},{16,18},{18... | collective-permute-start | bytes 5308424 | tf_op jit(solution)/shard_map/ppermute | solution.py:123
  72.5 44.1 %collective-permute-start.5 = (f32[24,6,8,384]{3,2,1,0:T(8,128)}, f32[24,6,8,384]{3,2,1,0:T(8,128)}, u32[]{:S(2)}, u32[]{:S(2)}) collective-permute-start(f32[24,6,8,384]{3,2,1,0:T(8,128)} %get-tuple-element.30), channel_id=1, source_target_pairs={{2,0},{4,2},{6,4},{8,6},{10,8},{12,10},{14,12},{16,14},{18,16},{20... | collective-permute-start | bytes 5308424 | tf_op jit(solution)/shard_map/ppermute | solution.py:123
  111.1 49.8 %collective-permute-start.6 = (f32[24,6,8,384]{3,2,1,0:T(8,128)}, f32[24,6,8,384]{3,2,1,0:T(8,128)S(1)}, u32[]{:S(2)}, u32[]{:S(2)}) collective-permute-start(f32[24,6,8,384]{3,2,1,0:T(8,128)} %get-tuple-element.29), channel_id=1, source_target_pairs={{0,2},{2,4},{4,6},{6,8},{8,10},{10,12},{12,14},{14,16},{16,18},{18... | collective-permute-start | bytes 5308424 | tf_op jit(solution)/shard_map/ppermute | solution.py:123
  115.2 45.7 %collective-permute-start.7 = (f32[24,6,8,384]{3,2,1,0:T(8,128)}, f32[24,6,8,384]{3,2,1,0:T(8,128)S(1)}, u32[]{:S(2)}, u32[]{:S(2)}) collective-permute-start(f32[24,6,8,384]{3,2,1,0:T(8,128)} %get-tuple-element.28), channel_id=1, source_target_pairs={{2,0},{4,2},{6,4},{8,6},{10,8},{12,10},{14,12},{16,14},{18,16},{20... | collective-permute-start | bytes 5308424 | tf_op jit(solution)/shard_map/ppermute | solution.py:123
  155.4 52.4 %collective-permute-start.8 = (f32[24,6,8,384]{3,2,1,0:T(8,128)}, f32[24,6,8,384]{3,2,1,0:T(8,128)S(1)}, u32[]{:S(2)}, u32[]{:S(2)}) collective-permute-start(f32[24,6,8,384]{3,2,1,0:T(8,128)} %get-tuple-element.27), channel_id=1, source_target_pairs={{0,2},{2,4},{4,6},{6,8},{8,10},{10,12},{12,14},{14,16},{16,18},{18... | collective-permute-start | bytes 5308424 | tf_op jit(solution)/shard_map/ppermute | solution.py:123
  159.6 51.9 %collective-permute-start.9 = (f32[24,6,8,384]{3,2,1,0:T(8,128)}, f32[24,6,8,384]{3,2,1,0:T(8,128)}, u32[]{:S(2)}, u32[]{:S(2)}) collective-permute-start(f32[24,6,8,384]{3,2,1,0:T(8,128)} %get-tuple-element.26), channel_id=1, source_target_pairs={{2,0},{4,2},{6,4},{8,6},{10,8},{12,10},{14,12},{16,14},{18,16},{20... | collective-permute-start | bytes 5308424 | tf_op jit(solution)/shard_map/ppermute | solution.py:123
  199.1 38.2 %collective-permute-start.10 = (f32[24,6,8,384]{3,2,1,0:T(8,128)}, f32[24,6,8,384]{3,2,1,0:T(8,128)}, u32[]{:S(2)}, u32[]{:S(2)}) collective-permute-start(f32[24,6,8,384]{3,2,1,0:T(8,128)} %get-tuple-element.25), channel_id=1, source_target_pairs={{0,2},{2,4},{4,6},{6,8},{8,10},{10,12},{12,14},{14,16},{16,18},{18... | collective-permute-start | bytes 5308424 | tf_op jit(solution)/shard_map/ppermute | solution.py:123
  204.5 36.8 %collective-permute-start.11 = (f32[24,6,8,384]{3,2,1,0:T(8,128)}, f32[24,6,8,384]{3,2,1,0:T(8,128)}, u32[]{:S(2)}, u32[]{:S(2)}) collective-permute-start(f32[24,6,8,384]{3,2,1,0:T(8,128)} %get-tuple-element.24), channel_id=1, source_target_pairs={{2,0},{4,2},{6,4},{8,6},{10,8},{12,10},{14,12},{16,14},{18,16},{20... | collective-permute-start | bytes 5308424 | tf_op jit(solution)/shard_map/ppermute | solution.py:123
  206.2 65.1 %collective-permute-start.12 = (f32[24,8,8,384]{3,2,1,0:T(8,128)}, f32[24,8,8,384]{3,2,1,0:T(8,128)}, u32[]{:S(2)}, u32[]{:S(2)}) collective-permute-start(f32[24,8,8,384]{3,2,1,0:T(8,128)} %shard_map.86), channel_id=1, source_target_pairs={{0,1},{1,0},{2,3},{3,2},{4,5},{5,4},{6,7},{7,6},{8,9},{9,8},{10,11... | collective-permute-start | bytes 7077896 | tf_op jit(solution)/shard_map/ppermute | solution.py:171
  209.0 102.1 %collective-permute-start.13 = (f32[24,8,8,384]{3,2,1,0:T(8,128)}, f32[24,8,8,384]{3,2,1,0:T(8,128)}, u32[]{:S(2)}, u32[]{:S(2)}) collective-permute-start(f32[24,8,8,384]{3,2,1,0:T(8,128)} %shard_map.87), channel_id=1, source_target_pairs={{0,1},{1,0},{2,3},{3,2},{4,5},{5,4},{6,7},{7,6},{8,9},{9,8},{10,11... | collective-permute-start | bytes 7077896 | tf_op jit(solution)/shard_map/ppermute | solution.py:171
  211.5 150.1 %collective-permute-start.14 = (f32[24,8,8,384]{3,2,1,0:T(8,128)}, f32[24,8,8,384]{3,2,1,0:T(8,128)}, u32[]{:S(2)}, u32[]{:S(2)}) collective-permute-start(f32[24,8,8,384]{3,2,1,0:T(8,128)} %copy-done.7), channel_id=1, source_target_pairs={{0,1},{1,0},{2,3},{3,2},{4,5},{5,4},{6,7},{7,6},{8,9},{9,8},{10,11... | collective-permute-start | bytes 7077896 | tf_op jit(solution)/shard_map/ppermute | solution.py:171
  237.3 174.9 %collective-permute-start.15 = (f32[24,8,8,384]{3,2,1,0:T(8,128)}, f32[24,8,8,384]{3,2,1,0:T(8,128)}, u32[]{:S(2)}, u32[]{:S(2)}) collective-permute-start(f32[24,8,8,384]{3,2,1,0:T(8,128)} %shard_map.89), channel_id=1, source_target_pairs={{0,1},{1,0},{2,3},{3,2},{4,5},{5,4},{6,7},{7,6},{8,9},{9,8},{10,11... | collective-permute-start | bytes 7077896 | tf_op jit(solution)/shard_map/ppermute | solution.py:171
  263.4 199.3 %collective-permute-start.16 = (f32[24,8,8,384]{3,2,1,0:T(8,128)S(1)}, f32[24,8,8,384]{3,2,1,0:T(8,128)S(1)}, u32[]{:S(2)}, u32[]{:S(2)}) collective-permute-start(f32[24,8,8,384]{3,2,1,0:T(8,128)S(1)} %shard_map.90), channel_id=1, source_target_pairs={{0,1},{1,0},{2,3},{3,2},{4,5},{5,4},{6,7},{7,6},{8,9},{9,8},{10,11... | collective-permute-start | bytes 7077896 | tf_op jit(solution)/shard_map/ppermute | solution.py:171
  484.2 17.7 %copy-start.11 = (f32[15,8,8,384]{3,2,1,0:T(8,128)S(1)}, f32[15,8,8,384]{3,2,1,0:T(8,128)}, u32[]{:S(2)}) copy-start(f32[15,8,8,384]{3,2,1,0:T(8,128)} %copy.31) | copy-start | bytes 4423684
  (17 other events, 89.3 us)
